TPU v7x, 32 devices: a whole 2x2x4 slice. The times are simulated.
32 devices in a mesh: pair: 4 (over z), aux: 8 (over y, x, core).
Axes of the slice: x: 2, y: 2, z: 4, core: 2. Of those that a mesh axis runs over, the one named last changes fastest.
Arguments:
- integrals: float32 [24, 128, 16, 128], P('pair', 'aux'), may hold values from -0.0034179688 to 0.0034179688
- mu_list: int32 [8, 24], P('aux', 'pair'), may hold values from 0 to 63, as said below
- lam_list: int32 [8, 24, 8], P('aux', 'pair'), may hold values from 0 to 63, as said below
- coeffs: float32 [64, 16, 64], replicated, may hold values from -6 to 6
- block_size: int32 [64], replicated, may hold values from 9 to 16
- block_order: int32 [64], replicated, may hold values from 0 to 63, as said below
Outputs:
- exchange: float32 [1024, 1024], P('pair', 'aux')
Inputs may be any that keep to these rules, and one draw needn't show every extreme that they name: `mu_list`: for every auxiliary index and every pair index, the 6 tiles of that device name row blocks whose owner pair index (block_order // 16) is shared by at most 2 of them, and some owner is named by exactly 2. `lam_list`: the 8 partner blocks of one tile are distinct. `block_order`: A permutation of the atom blocks.
All inputs are finite; a program needn't handle non-finite values.
Results may differ from a plain program's by a relative error of at most 0.0013.
Values may be sent and summed in bfloat16 or wider, within the bound.
A program may use at most 64 MiB of HBM per device.

v0:
```python
import jax
import jax.numpy as jnp
from jax import lax
from jax.sharding import PartitionSpec as P

CAP = 2


def crossed(left, right):
    return lax.dot_general(
        left, right, (((1,), (1,)), ((), ())), preferred_element_type=jnp.float32
    )


def body(integrals, mu_list, lam_list, coeffs, block_size, block_order):
    tiles = integrals.shape[0]
    aux_rows = integrals.shape[1]
    width = integrals.shape[2]
    nblk, _, nocc = coeffs.shape
    npair = lax.axis_size("pair")
    here = lax.axis_index("pair")
    blk_dev = nblk // npair
    ao_dev = blk_dev * width
    slot_count = npair * CAP
    span = jnp.arange(width, dtype=jnp.int32)
    live = (span[None, :] < block_size[:, None]).astype(jnp.float32)
    masked = coeffs * live[:, :, None]
    picked = masked[lam_list[0]].reshape(tiles, -1, nocc)
    half = jnp.einsum("tqmk,tki->tmqi", integrals, picked, precision=lax.Precision.HIGHEST)
    half = half.astype(jnp.bfloat16).reshape(tiles, width * aux_rows * nocc)
    place = block_order[mu_list[0]]
    owner = place // blk_dev
    local = place % blk_dev
    order_ids = jnp.arange(tiles, dtype=jnp.int32)
    earlier = (owner[None, :] == owner[:, None]) & (order_ids[None, :] < order_ids[:, None])
    rank = jnp.sum(earlier.astype(jnp.int32), axis=1)
    slot = owner * CAP + rank
    select = jnp.arange(slot_count, dtype=jnp.int32)[:, None] == slot[None, :]
    outgoing = jnp.dot(
        select.astype(jnp.bfloat16), half, preferred_element_type=jnp.float32
    ).astype(jnp.bfloat16)
    outgoing = outgoing.reshape(npair, CAP, width * aux_rows * nocc)
    labels = jnp.sum(jnp.where(select, local[None, :] + 1, 0), axis=1) - 1
    labels = labels.reshape(npair, CAP)
    incoming, labels_in = (
        lax.all_to_all(outgoing, "pair", split_axis=0, concat_axis=0, tiled=True),
        lax.all_to_all(labels, "pair", split_axis=0, concat_axis=0, tiled=True),
    )
    assign = (
        labels_in.reshape(-1)[None, :] == jnp.arange(blk_dev, dtype=jnp.int32)[:, None]
    ).astype(jnp.bfloat16)
    fitted = jnp.dot(assign, incoming.reshape(slot_count, -1), preferred_element_type=jnp.float32)
    fitted = fitted.astype(jnp.bfloat16).reshape(ao_dev, aux_rows * nocc)
    partial_value = crossed(fitted, lax.all_gather(fitted, "pair", axis=0, tiled=True))
    summed = lax.psum_scatter(partial_value, "aux", scatter_dimension=1, tiled=True)
    posmat = (block_order[None, :] == jnp.arange(nblk, dtype=jnp.int32)[:, None]).astype(
        jnp.float32
    )
    live_pos = jnp.dot(posmat, live, precision=lax.Precision.HIGHEST).reshape(-1)
    cols = summed.shape[1]
    row_mask = lax.dynamic_slice_in_dim(live_pos, here * ao_dev, ao_dev, 0)
    col_mask = lax.dynamic_slice_in_dim(live_pos, lax.axis_index("aux") * cols, cols, 0)
    return summed * row_mask[:, None] * col_mask[None, :]


def solution(mesh):
    return jax.shard_map(
        body,
        mesh=mesh,
        in_specs=(
            P("pair", "aux", None, None),
            P("aux", "pair"),
            P("aux", "pair", None),
            P(),
            P(),
            P(),
        ),
        out_specs=P("pair", "aux"),
        check_vma=False,
    )
```

profile of v0, /device:TPU:0, one launch (start us, length us, event | category | flops | bytes accessed | tf_op | source)
XLA Modules:
  0.0 128.7 jit_solution(15661634298438741537)
XLA Ops:
  6.5 0.7 fusion.10
  7.3 1.3 %gather_fusion = s32[6]{0:T(128)S(1)} fusion(s32[64]{0:T(128)} %param.11, s32[1024]{0:T(1024)S(1)} %pad_clamp_fusion.1), kind=kCustom, calls=%fused_computation | custom fusion | bytes 72 | tf_op jit(solution)/shard_map/gather | solution.py:31
  8.6 0.2 convert_reduce_fusion
  8.8 0.1 select_reduce_fusion
  8.9 0.7 sub.11
  9.6 6.3 %all-to-all-start = ((s32[4,1,2]{2,1,0:T(1,128)}), s32[4,1,2]{2,1,0:T(1,128)S(1)}, u32[]{:S(2)}, u32[]{:S(2)}) async-start(s32[4,1,2]{2,1,0:T(1,128)} %bitcast.2), calls=%async_computation | async-start | bytes 4096 | tf_op jit(solution)/shard_map/all_to_all | solution.py:47
  15.9 0.7 fusion.2
  16.6 0.7 fusion.7
  17.3 0.1 reshape.188
  17.4 1.2 broadcast_multiply_fusion
  18.7 0.6 gather_fusion.1
  19.3 0.8 fusion
  20.1 0.1 copy.17
  20.2 0.4 reshape.173
  20.6 0.2 convolution_convert_fusion.1
  20.8 0.9 reshape.174
  21.7 5.1 %all-to-all-start.1 = ((bf16[4,2,16384]{2,1,0:T(2,128)(2,1)}), bf16[4,2,16384]{2,1,0:T(2,128)(2,1)S(1)}, u32[]{:S(2)}, u32[]{:S(2)}) async-start(bf16[4,2,16384]{2,1,0:T(2,128)(2,1)} %reshape.174), calls=%async_computation.1 | async-start | bytes 524288 | tf_op jit(solution)/shard_map/all_to_all | solution.py:46
  26.7 0.5 broadcast.218
  27.3 0.7 reduce.5
  27.9 0.1 eq.62
  28.0 7.1 %all-to-all-done.1 = bf16[4,2,16384]{2,1,0:T(2,128)(2,1)S(1)} async-done(((bf16[4,2,16384]{2,1,0:T(2,128)(2,1)}), bf16[4,2,16384]{2,1,0:T(2,128)(2,1)S(1)}, u32[]{:S(2)}, u32[]{:S(2)}) %all-to-all-start.1) | async-done | bytes 262176 | tf_op jit(solution)/shard_map/all_to_all | solution.py:46
  35.1 0.1 reshape.175
  35.2 0.3 convolution_convert_fusion
  35.5 1.0 reshape.176
  36.6 45.1 %all-gather.2.cloned.1.call-done = bf16[1024,1024]{1,0:T(8,128)(2,1)} async-done(((bf16[256,1024]{1,0:T(8,128)(2,1)}), bf16[1024,1024]{1,0:T(8,128)(2,1)}) %all-gather.2.cloned.1.call-update) | async-done | bytes 2097168 | tf_op jit(solution)/shard_map/all_gather | solution.py:54
  81.7 3.5 %fusion.11 = f32[256,1024]{1,0:T(8,128)} fusion(bf16[256,1024]{1,0:T(8,128)(2,1)} %reshape.176, bf16[1024,1024]{1,0:T(8,128)(2,1)} %all-gather.2.cloned.1.call-done), kind=kOutput, calls=%fused_computation.36 | convolution fusion | flops 536870912 | bytes 3670016 | tf_op jit(solution)/shard_map/dot_general | solution.py:10
  85.3 0.2 fusion.1
  85.5 0.1 reshape.177
  85.5 0.1 dynamic_slice.6
  85.6 0.1 dynamic_slice.7
  85.7 34.5 %reduce-scatter.2.cloned.1.call-done = f32[256,128]{1,0:T(8,128)} async-done(((f32[256,1024]{1,0:T(8,128)}), f32[256,128]{1,0:T(8,128)}) %reduce-scatter.2.cloned.1.call-update) | async-done | bytes 131088 | tf_op jit(solution)/shard_map/reduce_scatter | solution.py:55
  120.2 1.7 %multiply_multiply_fusion = f32[256,128]{1,0:T(8,128)} fusion(f32[256,128]{1,0:T(8,128)} %reduce-scatter.2.cloned.1.call-done, f32[128]{0:T(128)S(1)} %dynamic_slice.7, f32[256]{0:T(256)S(1)} %dynamic_slice.6), kind=kLoop, calls=%fused_computation.7 | loop fusion | flops 65536 | bytes 263680 | tf_op jit(solution)/shard_map/mul | solution.py:63
  (16 shorter events, 0.1 us)
Async XLA Ops:
  6.5 12.7 %copy-start = (f32[6,16,16,128]{3,2,1,0:T(8,128)S(1)}, f32[6,16,16,128]{3,2,1,0:T(8,128)}, u32[]{:S(2)}) copy-start(f32[6,16,16,128]{3,2,1,0:T(8,128)} %param.6) | copy-start | bytes 2359300
  9.6 12.1 %all-to-all-start = ((s32[4,1,2]{2,1,0:T(1,128)}), s32[4,1,2]{2,1,0:T(1,128)S(1)}, u32[]{:S(2)}, u32[]{:S(2)}) async-start(s32[4,1,2]{2,1,0:T(1,128)} %bitcast.2), calls=%async_computation | async-start | bytes 4096 | tf_op jit(solution)/shard_map/all_to_all | solution.py:47
  21.7 13.4 %all-to-all-start.1 = ((bf16[4,2,16384]{2,1,0:T(2,128)(2,1)}), bf16[4,2,16384]{2,1,0:T(2,128)(2,1)S(1)}, u32[]{:S(2)}, u32[]{:S(2)}) async-start(bf16[4,2,16384]{2,1,0:T(2,128)(2,1)} %reshape.174), calls=%async_computation.1 | async-start | bytes 524288 | tf_op jit(solution)/shard_map/all_to_all | solution.py:46
  26.7 55.0 %all-gather.2.cloned.1.call-start = ((), (), s32[]{:S(2)}) async-start(), calls=%async_computation.3 | async-start | bytes 2621440 | tf_op jit(solution)/shard_map/all_gather | solution.py:54
  36.5 48.7 %copy-start.1 = (s32[64]{0:T(128)S(1)}, s32[64]{0:T(128)}, u32[]{:S(2)}) copy-start(s32[64]{0:T(128)} %param.11) | copy-start | bytes 772
  36.5 48.7 %copy-start.2 = (s32[64]{0:T(128)S(1)}, s32[64]{0:T(128)}, u32[]{:S(2)}) copy-start(s32[64]{0:T(128)} %param.10) | copy-start | bytes 772
  36.5 83.6 %reduce-scatter.2.cloned.1.call-start = ((), (), s32[]{:S(2)}) async-start(), calls=%async_computation.4 | async-start | bytes 1179648 | tf_op jit(solution)/shard_map/reduce_scatter | solution.py:55
Sparse Core Ops, SparseCore 0:
  36.6 45.0 all-gather.1
  85.4 34.7 reduce-scatter.1
where the time goes:
time: 129 us
  waiting for transfers between devices  86.7 us (67%)
  between operations  13.5 us (10%)
  starting transfers between devices  11.5 us (9%)
  other arithmetic  6.07 us (5%)
  local copies, waits for them, and re-layouts  5.97 us (5%)
  matrix products  4.96 us (4%)
    all_gather x1, waiting for transfers between devices, body(): lax.all_gather(fitted, 'pair', axis=0, tiled=True)  45.1 us
    reduce_scatter x1, waiting for transfers between devices, body(): lax.psum_scatter(partial_value, 'aux', scatter_dimension=1, tiled=True)  34.5 us
    all_to_all x1, waiting for transfers between devices, body(): lax.all_to_all(outgoing, 'pair', split_axis=0, concat_axis=0, tiled=True)  7.05 us
    all_to_all x1, starting transfers between devices, body(): lax.all_to_all(labels, 'pair', split_axis=0, concat_axis=0, tiled=True)  6.32 us
    all_to_all x1, starting transfers between devices, body(): lax.all_to_all(outgoing, 'pair', split_axis=0, concat_axis=0, tiled=True)  5.09 us
    dot_general x1, matrix products, crossed(): lax.dot_general(left, right, (((1,), (1,)), ((), ())), preferred_element_...  3.49 us
  transfers between devices with their start and end apart: 4, of which 3 were waited for; matrix products, arithmetic and copies ran while one was open for 6% of the time, Pallas kernels for 0%

commit v1 on v0

--- a/solution.py
+++ b/solution.py
@@ -1,9 +1,16 @@
+import functools
+
 import jax
 import jax.numpy as jnp
 from jax import lax
+from jax.experimental import pallas as pl
+from jax.experimental.pallas import tpu as pltpu
 from jax.sharding import PartitionSpec as P
 
 CAP = 2
+LANES = 128
+LABEL_ROWS = 8
+MESH = pl.DeviceIdType.MESH
 
 
 def crossed(left, right):
@@ -63,9 +70,269 @@
     return summed * row_mask[:, None] * col_mask[None, :]
 
 
+def mirrored(index, offset):
+    result = index
+    bit = 1
+    while bit <= offset:
+        if offset & bit:
+            result = result + bit * (1 - 2 * ((index // bit) % 2))
+        bit *= 2
+    return result
+
+
+def exchange_kernel(
+    npair, naux, mu_ref, lam_ref, size_ref, order_ref, integrals_ref, coeffs_ref, out_ref,
+    held, meta, sent, arrived, out_left, out_right, in_sem, meta_left, meta_right, meta_in, sum_out, sum_in,
+):
+    tiles, aux_rows, width, depth = integrals_ref.shape
+    nocc = coeffs_ref.shape[2]
+    partners = depth // width
+    ao_dev, cols = out_ref.shape
+    rows = tiles * width
+    padded = held.shape[1]
+    chunk = rows // 2
+    slot_rows = npair * CAP * width
+    here = lax.axis_index("pair")
+    column = lax.axis_index("aux")
+
+    barrier = pltpu.get_barrier_semaphore()
+
+    def greet(device):
+        pl.semaphore_signal(barrier, inc=1, device_id=device, device_id_type=MESH)
+
+    for offset in range(1, naux):
+        greet({"aux": mirrored(column, offset)})
+
+    @pl.when(here > 0)
+    def _():
+        greet({"pair": here - 1})
+
+    @pl.when(here < npair - 1)
+    def _():
+        greet({"pair": here + 1})
+
+    lane = lax.broadcasted_iota(jnp.int32, (LABEL_ROWS, LANES), 1)
+    places = [order_ref[mu_ref[0, t]] for t in range(tiles)]
+    target = jnp.full((LABEL_ROWS, LANES), -1, jnp.int32)
+    slots = jnp.full((LABEL_ROWS, LANES), -1, jnp.int32)
+    for t in range(tiles):
+        rank = jnp.int32(0)
+        for u in range(t):
+            rank = rank + (places[u] // (ao_dev // width) == places[t] // (ao_dev // width)).astype(jnp.int32)
+        mine = (lane >= t * width) & (lane < (t + 1) * width)
+        within = lane - t * width
+        target = jnp.where(mine, places[t] * width + within, target)
+        slots = jnp.where(mine, (here * CAP + rank) * width + within, slots)
+    meta[here, 0] = target
+    meta[here, 1] = slots
+
+    if padded > rows:
+        for layer in range(npair):
+            held[layer, rows:padded, :] = jnp.zeros((padded - rows, held.shape[2]), held.dtype)
+
+    row_in_block = lax.broadcasted_iota(jnp.int32, (width, nocc), 0)
+    packed = aux_rows // 2 * width
+    low_half = lax.broadcasted_iota(jnp.int32, (packed, 2 * nocc), 1) < nocc
+    row_in_tile = lax.broadcasted_iota(jnp.int32, (packed, 2 * nocc), 0) % width
+
+    def transform(t):
+        parts = []
+        for l in range(partners):
+            block = lam_ref[t, l]
+            parts.append(jnp.where(row_in_block < size_ref[block], coeffs_ref[block], 0.0))
+        picked = jnp.concatenate(parts, axis=0)
+        picked = jnp.concatenate([picked, picked], axis=1)
+        full = jnp.dot(
+            integrals_ref[t].reshape(aux_rows * width, depth), picked,
+            precision=lax.Precision.HIGHEST, preferred_element_type=jnp.float32,
+        )
+        half = jnp.where(low_half, full[:packed], full[packed:])
+        half = jnp.where(row_in_tile < size_ref[mu_ref[0, t]], half, 0.0).astype(held.dtype)
+        for j in range(aux_rows // 2):
+            held[here, t * width:(t + 1) * width, j * 2 * nocc:(j + 1) * 2 * nocc] = half[j * width:(j + 1) * width]
+
+    def move(layer, part, step):
+        sem = (out_left if step < 0 else out_right).at[layer, part]
+        piece = held.at[layer, pl.ds(part * chunk, chunk)]
+        return pltpu.make_async_remote_copy(
+            src_ref=piece, dst_ref=piece, send_sem=sem, recv_sem=in_sem.at[layer, part],
+            device_id={"pair": here + step}, device_id_type=MESH,
+        )
+
+    def move_meta(layer, step):
+        sem = (meta_left if step < 0 else meta_right).at[layer]
+        return pltpu.make_async_remote_copy(
+            src_ref=meta.at[layer], dst_ref=meta.at[layer], send_sem=sem, recv_sem=meta_in.at[layer],
+            device_id={"pair": here + step}, device_id_type=MESH,
+        )
+
+    def push(layer, part, step):
+        move(layer, part, step).start()
+        if part == 1:
+            move_meta(layer, step).start()
+
+    def take(layer, part, step):
+        move(layer, part, step).wait_recv()
+        if part == 1:
+            move_meta(layer, step).wait_recv()
+
+    for part in range(2):
+        for t in range(part * tiles // 2, (part + 1) * tiles // 2):
+            transform(t)
+        if part == 0:
+            before = (here + npair - 1) // npair
+            after = (2 * npair - 2 - here) // npair
+            pl.semaphore_wait(barrier, naux - 1 + before + after)
+
+        @pl.when(here < npair - 1)
+        def _():
+            push(here, part, 1)
+
+        @pl.when(here > 0)
+        def _():
+            push(here, part, -1)
+
+    for hops in range(1, npair):
+        for part in range(2):
+
+            @pl.when(here >= hops)
+            def _():
+                take(here - hops, part, -1)
+
+                @pl.when(here < npair - 1)
+                def _():
+                    push(here - hops, part, 1)
+
+            @pl.when(here + hops < npair)
+            def _():
+                take(here + hops, part, 1)
+
+                @pl.when(here > 0)
+                def _():
+                    push(here + hops, part, -1)
+
+    stacked = held[...].reshape(npair * padded, held.shape[2])
+    targets = jnp.concatenate([meta[k, 0, 0:1, :] for k in range(npair)], axis=1)
+    slotted = jnp.concatenate([meta[k, 1, 0:1, :] for k in range(npair)], axis=1)
+    first = here * ao_dev
+    slotted = jnp.where((targets >= first) & (targets < first + ao_dev), slotted, -1)
+    select = (
+        lax.broadcasted_iota(jnp.int32, (slot_rows, npair * padded), 0) == slotted
+    ).astype(jnp.float32).astype(jnp.bfloat16)
+    local = jnp.broadcast_to((targets - first + 1).astype(jnp.float32), (16, npair * padded)).astype(jnp.bfloat16)
+    local = jnp.where(slotted >= 0, local.astype(jnp.float32), 0.0).astype(jnp.bfloat16)
+    labels = lax.dot_general(local, select, (((1,), (1,)), ((), ())), preferred_element_type=jnp.float32)
+    labels = labels[:LABEL_ROWS]
+    owned = jnp.dot(select, stacked, preferred_element_type=jnp.float32).astype(jnp.bfloat16)
+    wanted = lax.broadcasted_iota(jnp.int32, (cols, npair * padded), 0)
+
+    def partial_sum(dest):
+        spread = (wanted + dest * cols == targets).astype(jnp.float32).astype(jnp.bfloat16)
+        fitted = jnp.dot(spread, stacked, preferred_element_type=jnp.float32).astype(jnp.bfloat16)
+        return lax.dot_general(owned, fitted, (((1,), (1,)), ((), ())), preferred_element_type=jnp.float32)
+
+    def ship(offset):
+        return pltpu.make_async_remote_copy(
+            src_ref=sent.at[offset], dst_ref=arrived.at[offset],
+            send_sem=sum_out.at[offset], recv_sem=sum_in.at[offset],
+            device_id={"aux": mirrored(column, offset)}, device_id_type=MESH,
+        )
+
+    out_row = (lax.broadcasted_iota(jnp.int32, (ao_dev, slot_rows), 0) + 1).astype(jnp.float32)
+
+    def place(label, value):
+        spread = (out_row == label).astype(jnp.float32).astype(jnp.bfloat16)
+        high = value.astype(jnp.bfloat16)
+        low = (value - high.astype(jnp.float32)).astype(jnp.bfloat16)
+        return jnp.dot(
+            jnp.concatenate([spread, spread], axis=1), jnp.concatenate([high, low], axis=0),
+            preferred_element_type=jnp.float32,
+        )
+
+    for offset in range(naux - 1, 0, -1):
+        sent[offset, :slot_rows] = partial_sum(mirrored(column, offset))
+        sent[offset, slot_rows:] = labels
+        ship(offset).start()
+    total = place(labels[0:1], partial_sum(column))
+    for offset in range(1, naux):
+        ship(offset).wait_recv()
+        total = total + place(arrived[offset, slot_rows:slot_rows + 1], arrived[offset, :slot_rows])
+    out_ref[...] = total
+
+    for offset in range(1, naux):
+        ship(offset).wait_send()
+    for layer in range(npair):
+        for part in range(2):
+
+            @pl.when((here < npair - 1) & (here >= layer))
+            def _():
+                move(layer, part, 1).wait_send()
+                if part == 1:
+                    move_meta(layer, 1).wait_send()
+
+            @pl.when((here > 0) & (here <= layer))
+            def _():
+                move(layer, part, -1).wait_send()
+                if part == 1:
+                    move_meta(layer, -1).wait_send()
+
+
+def fused(integrals, mu_list, lam_list, coeffs, block_size, block_order):
+    tiles, aux_rows, width, _ = integrals.shape
+    nblk, _, nocc = coeffs.shape
+    npair = lax.axis_size("pair")
+    naux = lax.axis_size("aux")
+    ao_dev = nblk // npair * width
+    cols = nblk * width // naux
+    summed_rows = npair * CAP * width + LABEL_ROWS
+    vmem = pl.BlockSpec(memory_space=pltpu.VMEM)
+    smem = pl.BlockSpec(memory_space=pltpu.SMEM)
+    dma = pltpu.SemaphoreType.DMA
+    return pl.pallas_call(
+        functools.partial(exchange_kernel, npair, naux),
+        out_shape=jax.ShapeDtypeStruct((ao_dev, cols), jnp.float32),
+        in_specs=[smem, smem, smem, smem, vmem, vmem],
+        out_specs=vmem,
+        scratch_shapes=[
+            pltpu.VMEM((npair, LANES, aux_rows * nocc), jnp.bfloat16),
+            pltpu.VMEM((npair, 2, LABEL_ROWS, LANES), jnp.int32),
+            pltpu.VMEM((naux, summed_rows, cols), jnp.float32),
+            pltpu.VMEM((naux, summed_rows, cols), jnp.float32),
+            dma((npair, 2)), dma((npair, 2)), dma((npair, 2)),
+            dma((npair,)), dma((npair,)), dma((npair,)),
+            dma((naux,)), dma((naux,)),
+        ],
+        compiler_params=pltpu.CompilerParams(
+            collective_id=0, has_side_effects=True, vmem_limit_bytes=48 * 1024 * 1024
+        ),
+    )(mu_list, lam_list[0], block_size, block_order, integrals, coeffs)
+
+
+def fits(integrals, mu_list, lam_list, coeffs, block_size, block_order):
+    tiles, aux_rows, width, depth = integrals.shape
+    nblk, _, nocc = coeffs.shape
+    npair = lax.axis_size("pair")
+    naux = lax.axis_size("aux")
+    return (
+        tiles % 2 == 0
+        and tiles * width <= LANES
+        and npair * CAP * width == LANES
+        and nblk * width // naux == LANES
+        and 2 * nocc == LANES
+        and aux_rows % 2 == 0
+        and width % 16 == 0
+        and nblk // npair * width <= 256
+        and naux & (naux - 1) == 0
+    )
+
+
+def device(*arrays):
+    return fused(*arrays) if fits(*arrays) else body(*arrays)
+
+
 def solution(mesh):
     return jax.shard_map(
-        body,
+        device,
         mesh=mesh,
         in_specs=(
             P("pair", "aux", None, None),

time: 129 us -> 34 us (0.26)
  waiting for transfers between devices: 86.7 us -> 0 us
  Pallas kernels: 0 us -> 29.6 us
  between operations: 13.5 us -> 0.01 us
  starting transfers between devices: 11.5 us -> 0 us
  other arithmetic: 6.07 us -> 0 us
  matrix products: 4.96 us -> 0 us
  local copies, waits for them, and re-layouts: 5.97 us -> 4.2 us
    all_gather x1 -> x0, waiting for transfers between devices: 45.1 us -> none  [body(): lax.all_gather(fitted, 'pair', axis=0, tiled=True)]
    reduce_scatter x1 -> x0, waiting for transfers between devices: 34.5 us -> none  [body(): lax.psum_scatter(partial_value, 'aux', scatter_dimension=1, tiled=True)]
    pallas_call x0 -> x1, Pallas kernels: none -> 29.6 us  [fused(): pl.pallas_call(functools.partial(exchange_kernel, npair, naux), out_shape...]
    all_to_all x2 -> x0, starting transfers between devices: 11.4 us -> none  [the longest x1 6.32 us: body(): lax.all_to_all(labels, 'pair', split_axis=0, concat_axis=0, tiled=True)]
    all_to_all x2 -> x0, waiting for transfers between devices: 7.06 us -> none  [the longest x1 7.05 us: body(): lax.all_to_all(outgoing, 'pair', split_axis=0, concat_axis=0, tiled=True)]
    dot_general x5 -> x0, matrix products: 4.96 us -> none  [the longest x1 3.49 us: crossed(): lax.dot_general(left, right, (((1,), (1,)), ((), ())), preferred_element_...]
    unnamed x6 -> x12, local copies, waits for them, and re-layouts: 0.02 us -> 4.2 us
    mul x2 -> x0, other arithmetic: 2.9 us -> none  [the longest x1 1.66 us: body(): return summed * row_mask[:, None] * col_mask[None, :]]
  transfers between devices with their start and end apart: 4 -> 0, of which waited for: 3 -> 0; matrix products, arithmetic and copies ran while one was open for 6% -> 0% of each run, Pallas kernels for 0% -> 0%
where the time goes in v1:
time: 34 us; the launch traced here: 33.8 us
  Pallas kernels  29.6 us (87%)
  local copies, waits for them, and re-layouts  4.2 us (12%)
    pallas_call x1, Pallas kernels, fused(): pl.pallas_call(functools.partial(exchange_kernel, npair, naux), out_shape...  29.6 us
    unnamed x12, local copies, waits for them, and re-layouts  4.2 us

profile of v1, /device:TPU:0, one launch (start us, length us, event | category | flops | bytes accessed | tf_op | source)
XLA Modules:
  0.0 33.8 jit_solution(3873535961369753639)
XLA Ops:
  0.0 0.7 %copy.9 = s32[1,6,8]{2,1,0:T(8,128)S(1)} copy(s32[1,6,8]{2,0,1:T(1,128)} %param.8) | data formatting | bytes 384
  0.7 0.0 copy-start.2
  0.7 0.0 copy-start.3
  0.7 0.0 copy-start.4
  0.7 0.6 %copy-done.2 = s32[1,6]{1,0:T(1,128)S(1)} copy-done((s32[1,6]{1,0:T(1,128)S(1)}, s32[1,6]{1,0:T(1,128)}, u32[]{:S(2)}) %copy-start.2) | copy-done | bytes 48
  1.3 0.0 copy-done.3
  1.4 0.0 copy-done.4
  1.4 0.0 copy-start
  1.4 1.1 %copy-done = f32[6,16,16,128]{3,2,1,0:T(8,128)S(1)} copy-done((f32[6,16,16,128]{3,2,1,0:T(8,128)S(1)}, f32[6,16,16,128]{3,2,1,0:T(8,128)}, u32[]{:S(2)}) %copy-start) | copy-done | bytes 786456
  2.5 0.0 copy-start.1
  2.5 1.0 %copy-done.1 = f32[64,16,64]{2,1,0:T(8,128)S(1)} copy-done((f32[64,16,64]{2,1,0:T(8,128)S(1)}, f32[64,16,64]{2,1,0:T(8,128)}, u32[]{:S(2)}) %copy-start.1) | copy-done | bytes 262168
  3.5 29.6 %shard_map.64 = f32[256,128]{1,0:T(8,128)S(1)} custom-call(s32[1,6]{1,0:T(1,128)S(1)} %copy-done.2, s32[6,8]{1,0:T(8,128)S(1)} %bitcast.3, s32[64]{0:T(128)S(1)} %copy-done.3, s32[64]{0:T(128)S(1)} %copy-done.4, f32[6,16,16,128]{3,2,1,0:T(8,128)S(1)} %copy-done, f32[64,16,64]{2,1,0:T(8,128)S(1)} %copy-done.1), custom_call_target="tpu_custom_call" | custom-call | tf_op jit(solution)/shard_map/pallas_call | solution.py:291
  33.2 0.7 %copy.11 = f32[256,128]{1,0:T(8,128)} copy(f32[256,128]{1,0:T(8,128)S(1)} %shard_map.64) | data formatting | bytes 262144
Async XLA Ops:
  0.7 0.7 %copy-start.2 = (s32[1,6]{1,0:T(1,128)S(1)}, s32[1,6]{1,0:T(1,128)}, u32[]{:S(2)}) copy-start(s32[1,6]{1,0:T(1,128)} %mu_ref.1) | copy-start | bytes 76
  0.7 0.7 %copy-start.3 = (s32[64]{0:T(128)S(1)}, s32[64]{0:T(128)}, u32[]{:S(2)}) copy-start(s32[64]{0:T(128)} %size_ref.1) | copy-start | bytes 772
  0.7 0.7 %copy-start.4 = (s32[64]{0:T(128)S(1)}, s32[64]{0:T(128)}, u32[]{:S(2)}) copy-start(s32[64]{0:T(128)} %order_ref.1) | copy-start | bytes 772
  1.4 1.1 %copy-start = (f32[6,16,16,128]{3,2,1,0:T(8,128)S(1)}, f32[6,16,16,128]{3,2,1,0:T(8,128)}, u32[]{:S(2)}) copy-start(f32[6,16,16,128]{3,2,1,0:T(8,128)} %integrals_ref.1) | copy-start | bytes 2359300
  2.5 1.0 %copy-start.1 = (f32[64,16,64]{2,1,0:T(8,128)S(1)}, f32[64,16,64]{2,1,0:T(8,128)}, u32[]{:S(2)}) copy-start(f32[64,16,64]{2,1,0:T(8,128)} %coeffs_ref.1) | copy-start | bytes 786436

commit v2 on v1

--- a/solution.py
+++ b/solution.py
@@ -81,8 +81,8 @@
 
 
 def exchange_kernel(
-    npair, naux, mu_ref, lam_ref, size_ref, order_ref, integrals_ref, coeffs_ref, out_ref,
-    held, meta, sent, arrived, out_left, out_right, in_sem, meta_left, meta_right, meta_in, sum_out, sum_in,
+    npair, naux, parts, mu_ref, lam_ref, size_ref, order_ref, integrals_hbm, coeffs_hbm, out_ref,
+    integrals_ref, coeffs_ref, load_sem, held, meta, sent, arrived, out_left, out_right, in_sem, meta_left, meta_right, meta_in, sum_out, sum_in,
 ):
     tiles, aux_rows, width, depth = integrals_ref.shape
     nocc = coeffs_ref.shape[2]
@@ -90,10 +90,19 @@
     ao_dev, cols = out_ref.shape
     rows = tiles * width
     padded = held.shape[1]
-    chunk = rows // 2
+    chunk = rows // parts
+    group = tiles // parts
     slot_rows = npair * CAP * width
     here = lax.axis_index("pair")
     column = lax.axis_index("aux")
+
+    coeffs_load = pltpu.make_async_copy(coeffs_hbm, coeffs_ref, load_sem.at[parts])
+    coeffs_load.start()
+    loads = []
+    for part in range(parts):
+        wanted = pl.ds(part * group, group)
+        loads.append(pltpu.make_async_copy(integrals_hbm.at[wanted], integrals_ref.at[wanted], load_sem.at[part]))
+        loads[part].start()
 
     barrier = pltpu.get_barrier_semaphore()
 
@@ -136,11 +145,11 @@
     row_in_tile = lax.broadcasted_iota(jnp.int32, (packed, 2 * nocc), 0) % width
 
     def transform(t):
-        parts = []
+        blocks = []
         for l in range(partners):
-            block = lam_ref[t, l]
-            parts.append(jnp.where(row_in_block < size_ref[block], coeffs_ref[block], 0.0))
-        picked = jnp.concatenate(parts, axis=0)
+            block = lam_ref[t, 0, l]
+            blocks.append(jnp.where(row_in_block < size_ref[block], coeffs_ref[block], 0.0))
+        picked = jnp.concatenate(blocks, axis=0)
         picked = jnp.concatenate([picked, picked], axis=1)
         full = jnp.dot(
             integrals_ref[t].reshape(aux_rows * width, depth), picked,
@@ -168,16 +177,18 @@
 
     def push(layer, part, step):
         move(layer, part, step).start()
-        if part == 1:
+        if part == parts - 1:
             move_meta(layer, step).start()
 
     def take(layer, part, step):
         move(layer, part, step).wait_recv()
-        if part == 1:
+        if part == parts - 1:
             move_meta(layer, step).wait_recv()
 
-    for part in range(2):
-        for t in range(part * tiles // 2, (part + 1) * tiles // 2):
+    coeffs_load.wait()
+    for part in range(parts):
+        loads[part].wait()
+        for t in range(part * group, (part + 1) * group):
             transform(t)
         if part == 0:
             before = (here + npair - 1) // npair
@@ -193,7 +204,7 @@
             push(here, part, -1)
 
     for hops in range(1, npair):
-        for part in range(2):
+        for part in range(parts):
 
             @pl.when(here >= hops)
             def _():
@@ -262,18 +273,18 @@
     for offset in range(1, naux):
         ship(offset).wait_send()
     for layer in range(npair):
-        for part in range(2):
+        for part in range(parts):
 
             @pl.when((here < npair - 1) & (here >= layer))
             def _():
                 move(layer, part, 1).wait_send()
-                if part == 1:
+                if part == parts - 1:
                     move_meta(layer, 1).wait_send()
 
             @pl.when((here > 0) & (here <= layer))
             def _():
                 move(layer, part, -1).wait_send()
-                if part == 1:
+                if part == parts - 1:
                     move_meta(layer, -1).wait_send()
 
 
@@ -288,24 +299,29 @@
     vmem = pl.BlockSpec(memory_space=pltpu.VMEM)
     smem = pl.BlockSpec(memory_space=pltpu.SMEM)
     dma = pltpu.SemaphoreType.DMA
+    anywhere = pl.BlockSpec(memory_space=pl.ANY)
+    parts = 3 if tiles % 3 == 0 else 1
     return pl.pallas_call(
-        functools.partial(exchange_kernel, npair, naux),
+        functools.partial(exchange_kernel, npair, naux, parts),
         out_shape=jax.ShapeDtypeStruct((ao_dev, cols), jnp.float32),
-        in_specs=[smem, smem, smem, smem, vmem, vmem],
+        in_specs=[smem, smem, smem, smem, anywhere, anywhere],
         out_specs=vmem,
         scratch_shapes=[
+            pltpu.VMEM(integrals.shape, jnp.float32),
+            pltpu.VMEM(coeffs.shape, jnp.float32),
+            dma((parts + 1,)),
             pltpu.VMEM((npair, LANES, aux_rows * nocc), jnp.bfloat16),
             pltpu.VMEM((npair, 2, LABEL_ROWS, LANES), jnp.int32),
             pltpu.VMEM((naux, summed_rows, cols), jnp.float32),
             pltpu.VMEM((naux, summed_rows, cols), jnp.float32),
-            dma((npair, 2)), dma((npair, 2)), dma((npair, 2)),
+            dma((npair, parts)), dma((npair, parts)), dma((npair, parts)),
             dma((npair,)), dma((npair,)), dma((npair,)),
             dma((naux,)), dma((naux,)),
         ],
         compiler_params=pltpu.CompilerParams(
-            collective_id=0, has_side_effects=True, vmem_limit_bytes=48 * 1024 * 1024
+            collective_id=0, has_side_effects=True, vmem_limit_bytes=60 * 1024 * 1024
         ),
-    )(mu_list, lam_list[0], block_size, block_order, integrals, coeffs)
+    )(mu_list, jnp.transpose(lam_list, (1, 0, 2)), block_size, block_order, integrals, coeffs)
 
 
 def fits(integrals, mu_list, lam_list, coeffs, block_size, block_order):
@@ -314,8 +330,7 @@
     npair = lax.axis_size("pair")
     naux = lax.axis_size("aux")
     return (
-        tiles % 2 == 0
-        and tiles * width <= LANES
+        tiles * width <= LANES
         and npair * CAP * width == LANES
         and nblk * width // naux == LANES
         and 2 * nocc == LANES

time: 34 us -> 31.9 us (0.938)
  local copies, waits for them, and re-layouts: 4.2 us -> 1.57 us
  Pallas kernels: 29.6 us -> 30.2 us
    unnamed x12 -> x1, local copies, waits for them, and re-layouts: 4.2 us -> 1.57 us
    pallas_call x1, Pallas kernels: 29.6 us -> 30.2 us  [fused(): pl.pallas_call(functools.partial(exchange_kernel, npair, naux, parts), ou...]
where the time goes in v2:
time: 31.9 us; the launch traced here: 31.7 us
  Pallas kernels  30.2 us (95%)
  local copies, waits for them, and re-layouts  1.57 us (5%)
    pallas_call x1, Pallas kernels, fused(): pl.pallas_call(functools.partial(exchange_kernel, npair, naux, parts), ou...  30.2 us
    unnamed x1, local copies, waits for them, and re-layouts  1.57 us

profile of v2, /device:TPU:0, one launch (start us, length us, event | category | flops | bytes accessed | tf_op | source)
XLA Modules:
  0.0 31.7 jit_solution(16343886511901364958)
XLA Ops:
  0.0 30.2 %shard_map.64 = f32[256,128]{1,0:T(8,128)} custom-call(s32[1,6]{1,0:T(1,128)} %mu_ref.1, s32[6,1,8]{2,1,0:T(1,128)} %bitcast.1, s32[64]{0:T(128)} %size_ref.1, s32[64]{0:T(128)} %order_ref.1, f32[6,16,16,128]{3,2,1,0:T(8,128)} %integrals_hbm.1, f32[64,16,64]{2,1,0:T(8,128)} %coeffs_hbm.1), custom_call_target="tpu_custom_call" | custom-call | tf_op jit(solution)/shard_map/pallas_call | solution.py:304
  30.2 1.6 %copy.8 = f32[256,128]{1,0:T(8,128)} copy(f32[256,128]{1,0:T(8,128)} %shard_map.64) | data formatting | bytes 262144

commit v3 on v2

--- a/solution.py
+++ b/solution.py
@@ -81,8 +81,8 @@
 
 
 def exchange_kernel(
-    npair, naux, parts, mu_ref, lam_ref, size_ref, order_ref, integrals_hbm, coeffs_hbm, out_ref,
-    integrals_ref, coeffs_ref, load_sem, held, meta, sent, arrived, out_left, out_right, in_sem, meta_left, meta_right, meta_in, sum_out, sum_in,
+    npair, naux, parts, mu_hbm, lam_hbm, size_hbm, order_hbm, integrals_hbm, coeffs_hbm, out_ref,
+    mu_ref, lam_ref, size_ref, order_ref, scalar_sem, integrals_ref, coeffs_ref, load_sem, held, meta, sent, arrived, out_left, out_right, in_sem, meta_left, meta_right, meta_in, sum_out, sum_in,
 ):
     tiles, aux_rows, width, depth = integrals_ref.shape
     nocc = coeffs_ref.shape[2]
@@ -95,7 +95,13 @@
     slot_rows = npair * CAP * width
     here = lax.axis_index("pair")
     column = lax.axis_index("aux")
-
+    low_layer = here < npair // 2
+    high_layer = here >= npair // 2
+
+    scalar_loads = []
+    for source, dest in ((mu_hbm, mu_ref), (lam_hbm, lam_ref), (size_hbm, size_ref), (order_hbm, order_ref)):
+        scalar_loads.append(pltpu.make_async_copy(source, dest, scalar_sem.at[len(scalar_loads)]))
+        scalar_loads[-1].start()
     coeffs_load = pltpu.make_async_copy(coeffs_hbm, coeffs_ref, load_sem.at[parts])
     coeffs_load.start()
     loads = []
@@ -120,6 +126,8 @@
     def _():
         greet({"pair": here + 1})
 
+    for load in scalar_loads:
+        load.wait()
     lane = lax.broadcasted_iota(jnp.int32, (LABEL_ROWS, LANES), 1)
     places = [order_ref[mu_ref[0, t]] for t in range(tiles)]
     target = jnp.full((LABEL_ROWS, LANES), -1, jnp.int32)
@@ -195,32 +203,40 @@
             after = (2 * npair - 2 - here) // npair
             pl.semaphore_wait(barrier, naux - 1 + before + after)
 
+        @pl.when((here > 0) & low_layer)
+        def _():
+            push(here, part, -1)
+
         @pl.when(here < npair - 1)
         def _():
             push(here, part, 1)
 
-        @pl.when(here > 0)
+        @pl.when((here > 0) & high_layer)
         def _():
             push(here, part, -1)
 
+    def pass_on(hops, part, step):
+        take(here + step * hops, part, step)
+        onward = here > 0 if step > 0 else here < npair - 1
+
+        @pl.when(onward)
+        def _():
+            push(here + step * hops, part, step * -1)
+
     for hops in range(1, npair):
         for part in range(parts):
 
+            @pl.when((here + hops < npair) & low_layer)
+            def _():
+                pass_on(hops, part, 1)
+
             @pl.when(here >= hops)
             def _():
-                take(here - hops, part, -1)
-
-                @pl.when(here < npair - 1)
-                def _():
-                    push(here - hops, part, 1)
-
-            @pl.when(here + hops < npair)
-            def _():
-                take(here + hops, part, 1)
-
-                @pl.when(here > 0)
-                def _():
-                    push(here + hops, part, -1)
+                pass_on(hops, part, -1)
+
+            @pl.when((here + hops < npair) & high_layer)
+            def _():
+                pass_on(hops, part, 1)
 
     stacked = held[...].reshape(npair * padded, held.shape[2])
     targets = jnp.concatenate([meta[k, 0, 0:1, :] for k in range(npair)], axis=1)
@@ -297,16 +313,20 @@
     cols = nblk * width // naux
     summed_rows = npair * CAP * width + LABEL_ROWS
     vmem = pl.BlockSpec(memory_space=pltpu.VMEM)
-    smem = pl.BlockSpec(memory_space=pltpu.SMEM)
     dma = pltpu.SemaphoreType.DMA
-    anywhere = pl.BlockSpec(memory_space=pl.ANY)
+    hbm = pl.BlockSpec(memory_space=pltpu.HBM)
     parts = 3 if tiles % 3 == 0 else 1
     return pl.pallas_call(
         functools.partial(exchange_kernel, npair, naux, parts),
         out_shape=jax.ShapeDtypeStruct((ao_dev, cols), jnp.float32),
-        in_specs=[smem, smem, smem, smem, anywhere, anywhere],
+        in_specs=[hbm] * 6,
         out_specs=vmem,
         scratch_shapes=[
+            pltpu.SMEM(mu_list.shape, jnp.int32),
+            pltpu.SMEM((tiles, 1, lam_list.shape[2]), jnp.int32),
+            pltpu.SMEM(block_size.shape, jnp.int32),
+            pltpu.SMEM(block_order.shape, jnp.int32),
+            dma((4,)),
             pltpu.VMEM(integrals.shape, jnp.float32),
             pltpu.VMEM(coeffs.shape, jnp.float32),
             dma((parts + 1,)),

time: 31.9 us -> 31.2 us (0.978)
  Pallas kernels: 30.2 us -> 29.4 us
    pallas_call x1, Pallas kernels: 30.2 us -> 29.4 us  [fused(): pl.pallas_call(functools.partial(exchange_kernel, npair, naux, parts), ou...]
where the time goes in v3:
time: 31.2 us; the launch traced here: 31 us
  Pallas kernels  29.4 us (94%)
  local copies, waits for them, and re-layouts  1.57 us (5%)
    pallas_call x1, Pallas kernels, fused(): pl.pallas_call(functools.partial(exchange_kernel, npair, naux, parts), ou...  29.4 us
    unnamed x1, local copies, waits for them, and re-layouts  1.57 us

profile of v3, /device:TPU:0, one launch (start us, length us, event | category | flops | bytes accessed | tf_op | source)
XLA Modules:
  0.0 31.0 jit_solution(17494396152207354699)
XLA Ops:
  0.0 29.4 %shard_map.64 = f32[256,128]{1,0:T(8,128)} custom-call(s32[1,6]{1,0:T(1,128)} %mu_hbm.1, s32[6,1,8]{2,1,0:T(1,128)} %bitcast.1, s32[64]{0:T(128)} %size_hbm.1, s32[64]{0:T(128)} %order_hbm.1, f32[6,16,16,128]{3,2,1,0:T(8,128)} %integrals_hbm.1, f32[64,16,64]{2,1,0:T(8,128)} %coeffs_hbm.1), custom_call_target="tpu_custom_call" | custom-call | tf_op jit(solution)/shard_map/pallas_call | solution.py:319
  29.5 1.6 %copy.8 = f32[256,128]{1,0:T(8,128)} copy(f32[256,128]{1,0:T(8,128)} %shard_map.64) | data formatting | bytes 262144

commit v4 on v3

--- a/solution.py
+++ b/solution.py
@@ -82,7 +82,8 @@
 
 def exchange_kernel(
     npair, naux, parts, mu_hbm, lam_hbm, size_hbm, order_hbm, integrals_hbm, coeffs_hbm, out_ref,
-    mu_ref, lam_ref, size_ref, order_ref, scalar_sem, integrals_ref, coeffs_ref, load_sem, held, meta, sent, arrived, out_left, out_right, in_sem, meta_left, meta_right, meta_in, sum_out, sum_in,
+    mu_ref, lam_ref, size_ref, order_ref, scalar_sem, integrals_ref, coeffs_ref, load_sem, held, meta, near_fitted, sent_near, near_in, sent_far, far_in, out_left, out_right, in_sem, meta_left, meta_right, meta_in,
+    near_out, near_arrived, far_out, far_arrived,
 ):
     tiles, aux_rows, width, depth = integrals_ref.shape
     nocc = coeffs_ref.shape[2]
@@ -92,7 +93,6 @@
     padded = held.shape[1]
     chunk = rows // parts
     group = tiles // parts
-    slot_rows = npair * CAP * width
     here = lax.axis_index("pair")
     column = lax.axis_index("aux")
     low_layer = here < npair // 2
@@ -223,7 +223,7 @@
         def _():
             push(here + step * hops, part, step * -1)
 
-    for hops in range(1, npair):
+    def gather_step(hops):
         for part in range(parts):
 
             @pl.when((here + hops < npair) & low_layer)
@@ -238,56 +238,114 @@
             def _():
                 pass_on(hops, part, 1)
 
-    stacked = held[...].reshape(npair * padded, held.shape[2])
-    targets = jnp.concatenate([meta[k, 0, 0:1, :] for k in range(npair)], axis=1)
-    slotted = jnp.concatenate([meta[k, 1, 0:1, :] for k in range(npair)], axis=1)
-    first = here * ao_dev
-    slotted = jnp.where((targets >= first) & (targets < first + ao_dev), slotted, -1)
-    select = (
-        lax.broadcasted_iota(jnp.int32, (slot_rows, npair * padded), 0) == slotted
-    ).astype(jnp.float32).astype(jnp.bfloat16)
-    local = jnp.broadcast_to((targets - first + 1).astype(jnp.float32), (16, npair * padded)).astype(jnp.bfloat16)
-    local = jnp.where(slotted >= 0, local.astype(jnp.float32), 0.0).astype(jnp.bfloat16)
-    labels = lax.dot_general(local, select, (((1,), (1,)), ((), ())), preferred_element_type=jnp.float32)
-    labels = labels[:LABEL_ROWS]
-    owned = jnp.dot(select, stacked, preferred_element_type=jnp.float32).astype(jnp.bfloat16)
-    wanted = lax.broadcasted_iota(jnp.int32, (cols, npair * padded), 0)
-
-    def partial_sum(dest):
-        spread = (wanted + dest * cols == targets).astype(jnp.float32).astype(jnp.bfloat16)
-        fitted = jnp.dot(spread, stacked, preferred_element_type=jnp.float32).astype(jnp.bfloat16)
-        return lax.dot_general(owned, fitted, (((1,), (1,)), ((), ())), preferred_element_type=jnp.float32)
-
-    def ship(offset):
+    def one_hot(rows_of, wanted_row):
+        found = lax.broadcasted_iota(jnp.int32, (rows_of, wanted_row.shape[1]), 0) == wanted_row
+        return found.astype(jnp.float32).astype(jnp.bfloat16)
+
+    def times(left, right):
+        return jnp.dot(left, right, preferred_element_type=jnp.float32)
+
+    def label_row(local, select):
+        local = jnp.broadcast_to(local.astype(jnp.float32), (16, local.shape[1])).astype(jnp.bfloat16)
+        return crossed(local, select)[:LABEL_ROWS]
+
+    def ship(source, dest, out_sems, in_sems, offset):
         return pltpu.make_async_remote_copy(
-            src_ref=sent.at[offset], dst_ref=arrived.at[offset],
-            send_sem=sum_out.at[offset], recv_sem=sum_in.at[offset],
+            src_ref=source.at[offset], dst_ref=dest.at[offset],
+            send_sem=out_sems.at[offset], recv_sem=in_sems.at[offset],
             device_id={"aux": mirrored(column, offset)}, device_id_type=MESH,
         )
 
-    out_row = (lax.broadcasted_iota(jnp.int32, (ao_dev, slot_rows), 0) + 1).astype(jnp.float32)
-
-    def place(label, value):
-        spread = (out_row == label).astype(jnp.float32).astype(jnp.bfloat16)
+    def ship_near(offset):
+        return ship(sent_near, near_in, near_out, near_arrived, offset)
+
+    def ship_far(offset):
+        return ship(sent_far, far_in, far_out, far_arrived, offset)
+
+    for hops in range(1, npair - 1):
+        gather_step(hops)
+
+    upper = here // (npair // 2)
+    far = (npair - 1) * (1 - upper)
+    layers = npair - 1
+    slots_of = CAP * width
+    near_rows = layers * slots_of
+    first = here * ao_dev
+
+    near = held[pl.ds(upper, layers)].reshape(layers * padded, held.shape[2])
+    near_targets = jnp.concatenate([meta[upper + k, 0, 0:1, :] for k in range(layers)], axis=1)
+    near_slots = jnp.concatenate([meta[upper + k, 1, 0:1, :] for k in range(layers)], axis=1)
+    near_mine = (near_targets >= first) & (near_targets < first + ao_dev)
+    near_slots = jnp.where(near_mine, near_slots - upper * slots_of, -1)
+    near_select = one_hot(LANES, near_slots)
+    near_labels = label_row(jnp.where(near_mine, near_targets - first + 1, 0), near_select)
+    near_owned = times(near_select, near).astype(jnp.bfloat16)
+    for offset in range(naux - 1, -1, -1):
+        fitted = times(one_hot(cols, near_targets - mirrored(column, offset) * cols), near).astype(jnp.bfloat16)
+        near_fitted[offset] = fitted
+        sent_near[offset, :near_rows] = crossed(near_owned, fitted)[:near_rows]
+        sent_near[offset, near_rows:] = near_labels
+        if offset:
+            ship_near(offset).start()
+
+    gather_step(npair - 1)
+
+    last = held[far]
+    far_targets = meta[far, 0, 0:1, :]
+    far_ranks = meta[far, 1, 0:1, :] - far * slots_of
+    far_mine = (far_targets >= first) & (far_targets < first + ao_dev)
+    far_select = one_hot(slots_of, jnp.where(far_mine, far_ranks, -1))
+    far_select_wide = one_hot(LANES, jnp.where(far_mine, far_ranks, -1))
+    far_labels = label_row(jnp.where(far_mine, far_targets - first + 1, 0), far_select_wide)
+    far_owned = times(far_select, last).astype(jnp.bfloat16)
+    top_row = lax.broadcasted_iota(jnp.int32, (LABEL_ROWS, LANES), 0) == 0
+    for offset in range(naux - 1, -1, -1):
+        shifted = far_targets - mirrored(column, offset) * cols
+        inside = (shifted >= 0) & (shifted < cols)
+        ranks = jnp.where(inside, far_ranks, -1)
+        moved = times(one_hot(slots_of, ranks), last).astype(jnp.bfloat16)
+        column_labels = label_row(jnp.where(inside, shifted + 1, 0), one_hot(LANES, ranks))
+        fitted = times(one_hot(cols, shifted), last).astype(jnp.bfloat16)
+        sent_far[offset, :slots_of] = crossed(far_owned, near_fitted[offset]) + crossed(far_owned, fitted)
+        sent_far[offset, slots_of:2 * slots_of] = crossed(moved, near_owned)
+        sent_far[offset, 2 * slots_of:] = jnp.where(top_row, far_labels, column_labels)
+        if offset:
+            ship_far(offset).start()
+
+    def split(value):
         high = value.astype(jnp.bfloat16)
-        low = (value - high.astype(jnp.float32)).astype(jnp.bfloat16)
-        return jnp.dot(
-            jnp.concatenate([spread, spread], axis=1), jnp.concatenate([high, low], axis=0),
-            preferred_element_type=jnp.float32,
-        )
-
-    for offset in range(naux - 1, 0, -1):
-        sent[offset, :slot_rows] = partial_sum(mirrored(column, offset))
-        sent[offset, slot_rows:] = labels
-        ship(offset).start()
-    total = place(labels[0:1], partial_sum(column))
+        return high, (value - high.astype(jnp.float32)).astype(jnp.bfloat16)
+
+    def spread(count, label):
+        row = (lax.broadcasted_iota(jnp.int32, (count, label.shape[1]), 0) + 1).astype(jnp.float32)
+        return (row == label).astype(jnp.float32).astype(jnp.bfloat16)
+
+    total = jnp.zeros((ao_dev, cols), jnp.float32)
+    for offset in range(naux):
+        if offset:
+            ship_near(offset).wait_recv()
+        source = near_in if offset else sent_near
+        rows_near = spread(ao_dev, source[offset, near_rows:near_rows + 1, :])
+        high, low = split(source[offset, :near_rows])
+        total = total + times(rows_near[:, :near_rows], high) + times(rows_near[:, :near_rows], low)
+    for offset in range(naux):
+        if offset:
+            ship_far(offset).wait_recv()
+        near_source = near_in if offset else sent_near
+        source = far_in if offset else sent_far
+        rows_near = spread(ao_dev, near_source[offset, near_rows:near_rows + 1, :])
+        rows_far = spread(ao_dev, source[offset, 2 * slots_of:2 * slots_of + 1, :slots_of])
+        cols_far = spread(cols, source[offset, 2 * slots_of + 1:2 * slots_of + 2, :slots_of])
+        high, low = split(source[offset, :slots_of])
+        total = total + times(rows_far, high) + times(rows_far, low)
+        high, low = split(source[offset, slots_of:2 * slots_of])
+        high, low = split(times(cols_far, high) + times(cols_far, low))
+        total = total + crossed(rows_near, high) + crossed(rows_near, low)
+    out_ref[...] = total
+
     for offset in range(1, naux):
-        ship(offset).wait_recv()
-        total = total + place(arrived[offset, slot_rows:slot_rows + 1], arrived[offset, :slot_rows])
-    out_ref[...] = total
-
-    for offset in range(1, naux):
-        ship(offset).wait_send()
+        ship_near(offset).wait_send()
+        ship_far(offset).wait_send()
     for layer in range(npair):
         for part in range(parts):
 
@@ -311,7 +369,8 @@
     naux = lax.axis_size("aux")
     ao_dev = nblk // npair * width
     cols = nblk * width // naux
-    summed_rows = npair * CAP * width + LABEL_ROWS
+    near_rows = (npair - 1) * CAP * width + LABEL_ROWS
+    far_rows = 2 * CAP * width + LABEL_ROWS
     vmem = pl.BlockSpec(memory_space=pltpu.VMEM)
     dma = pltpu.SemaphoreType.DMA
     hbm = pl.BlockSpec(memory_space=pltpu.HBM)
@@ -332,11 +391,14 @@
             dma((parts + 1,)),
             pltpu.VMEM((npair, LANES, aux_rows * nocc), jnp.bfloat16),
             pltpu.VMEM((npair, 2, LABEL_ROWS, LANES), jnp.int32),
-            pltpu.VMEM((naux, summed_rows, cols), jnp.float32),
-            pltpu.VMEM((naux, summed_rows, cols), jnp.float32),
+            pltpu.VMEM((naux, cols, aux_rows * nocc), jnp.bfloat16),
+            pltpu.VMEM((naux, near_rows, cols), jnp.float32),
+            pltpu.VMEM((naux, near_rows, cols), jnp.float32),
+            pltpu.VMEM((naux, far_rows, cols), jnp.float32),
+            pltpu.VMEM((naux, far_rows, cols), jnp.float32),
             dma((npair, parts)), dma((npair, parts)), dma((npair, parts)),
             dma((npair,)), dma((npair,)), dma((npair,)),
-            dma((naux,)), dma((naux,)),
+            dma((naux,)), dma((naux,)), dma((naux,)), dma((naux,)),
         ],
         compiler_params=pltpu.CompilerParams(
             collective_id=0, has_side_effects=True, vmem_limit_bytes=60 * 1024 * 1024
@@ -356,6 +418,7 @@
         and 2 * nocc == LANES
         and aux_rows % 2 == 0
         and width % 16 == 0
+        and npair % 2 == 0
         and nblk // npair * width <= 256
         and naux & (naux - 1) == 0
     )

time: 31.2 us -> 29.5 us (0.946)
  Pallas kernels: 29.4 us -> 27.8 us
    pallas_call x1, Pallas kernels: 29.4 us -> 27.8 us  [fused(): pl.pallas_call(functools.partial(exchange_kernel, npair, naux, parts), ou...]
where the time goes in v4:
time: 29.5 us; the launch traced here: 29.4 us
  Pallas kernels  27.8 us (94%)
  local copies, waits for them, and re-layouts  1.57 us (5%)
    pallas_call x1, Pallas kernels, fused(): pl.pallas_call(functools.partial(exchange_kernel, npair, naux, parts), ou...  27.8 us
    unnamed x1, local copies, waits for them, and re-layouts  1.57 us

profile of v4, /device:TPU:0, one launch (start us, length us, event | category | flops | bytes accessed | tf_op | source)
XLA Modules:
  0.0 29.4 jit_solution(2576368948970994829)
XLA Ops:
  0.0 27.8 %shard_map.64 = f32[256,128]{1,0:T(8,128)} custom-call(s32[1,6]{1,0:T(1,128)} %mu_hbm.1, s32[6,1,8]{2,1,0:T(1,128)} %bitcast.1, s32[64]{0:T(128)} %size_hbm.1, s32[64]{0:T(128)} %order_hbm.1, f32[6,16,16,128]{3,2,1,0:T(8,128)} %integrals_hbm.1, f32[64,16,64]{2,1,0:T(8,128)} %coeffs_hbm.1), custom_call_target="tpu_custom_call" | custom-call | tf_op jit(solution)/shard_map/pallas_call | solution.py:378
  27.8 1.6 %copy.8 = f32[256,128]{1,0:T(8,128)} copy(f32[256,128]{1,0:T(8,128)} %shard_map.64) | data formatting | bytes 262144

commit v5 on v4

--- a/solution.py
+++ b/solution.py
@@ -249,6 +249,10 @@
         local = jnp.broadcast_to(local.astype(jnp.float32), (16, local.shape[1])).astype(jnp.bfloat16)
         return crossed(local, select)[:LABEL_ROWS]
 
+    def split(value):
+        high = value.astype(jnp.bfloat16)
+        return high, (value - high.astype(jnp.float32)).astype(jnp.bfloat16)
+
     def ship(source, dest, out_sems, in_sems, offset):
         return pltpu.make_async_remote_copy(
             src_ref=source.at[offset], dst_ref=dest.at[offset],
@@ -298,23 +302,23 @@
     far_select_wide = one_hot(LANES, jnp.where(far_mine, far_ranks, -1))
     far_labels = label_row(jnp.where(far_mine, far_targets - first + 1, 0), far_select_wide)
     far_owned = times(far_select, last).astype(jnp.bfloat16)
+    own_high, own_low = split(crossed(far_owned, last))
+    far_high, far_low = split(crossed(last, near_owned))
     top_row = lax.broadcasted_iota(jnp.int32, (LABEL_ROWS, LANES), 0) == 0
     for offset in range(naux - 1, -1, -1):
         shifted = far_targets - mirrored(column, offset) * cols
         inside = (shifted >= 0) & (shifted < cols)
         ranks = jnp.where(inside, far_ranks, -1)
-        moved = times(one_hot(slots_of, ranks), last).astype(jnp.bfloat16)
         column_labels = label_row(jnp.where(inside, shifted + 1, 0), one_hot(LANES, ranks))
-        fitted = times(one_hot(cols, shifted), last).astype(jnp.bfloat16)
-        sent_far[offset, :slots_of] = crossed(far_owned, near_fitted[offset]) + crossed(far_owned, fitted)
-        sent_far[offset, slots_of:2 * slots_of] = crossed(moved, near_owned)
+        moved = one_hot(slots_of, ranks)
+        spot = one_hot(cols, shifted)
+        sent_far[offset, :slots_of] = (
+            crossed(far_owned, near_fitted[offset]) + crossed(own_high, spot) + crossed(own_low, spot)
+        )
+        sent_far[offset, slots_of:2 * slots_of] = times(moved, far_high) + times(moved, far_low)
         sent_far[offset, 2 * slots_of:] = jnp.where(top_row, far_labels, column_labels)
         if offset:
             ship_far(offset).start()
-
-    def split(value):
-        high = value.astype(jnp.bfloat16)
-        return high, (value - high.astype(jnp.float32)).astype(jnp.bfloat16)
 
     def spread(count, label):
         row = (lax.broadcasted_iota(jnp.int32, (count, label.shape[1]), 0) + 1).astype(jnp.float32)

time: 29.5 us -> 29.4 us (level)
  no operation moved by 1% of the time
where the time goes in v5:
time: 29.4 us; the launch traced here: 29.3 us
  Pallas kernels  27.7 us (94%)
  local copies, waits for them, and re-layouts  1.57 us (5%)
    pallas_call x1, Pallas kernels, fused(): pl.pallas_call(functools.partial(exchange_kernel, npair, naux, parts), ou...  27.7 us
    unnamed x1, local copies, waits for them, and re-layouts  1.57 us

profile of v5, /device:TPU:0, one launch (start us, length us, event | category | flops | bytes accessed | tf_op | source)
XLA Modules:
  0.0 29.3 jit_solution(18183991685565127058)
XLA Ops:
  0.0 27.7 %shard_map.64 = f32[256,128]{1,0:T(8,128)} custom-call(s32[1,6]{1,0:T(1,128)} %mu_hbm.1, s32[6,1,8]{2,1,0:T(1,128)} %bitcast.1, s32[64]{0:T(128)} %size_hbm.1, s32[64]{0:T(128)} %order_hbm.1, f32[6,16,16,128]{3,2,1,0:T(8,128)} %integrals_hbm.1, f32[64,16,64]{2,1,0:T(8,128)} %coeffs_hbm.1), custom_call_target="tpu_custom_call" | custom-call | tf_op jit(solution)/shard_map/pallas_call | solution.py:382
  27.7 1.6 %copy.8 = f32[256,128]{1,0:T(8,128)} copy(f32[256,128]{1,0:T(8,128)} %shard_map.64) | data formatting | bytes 262144

commit v6 on v4

--- a/solution.py
+++ b/solution.py
@@ -223,6 +223,9 @@
         def _():
             push(here + step * hops, part, step * -1)
 
+    send_order = sorted(range(naux), key=lambda offset: (-(offset % 2), -offset))
+    send_order = [offset for offset in send_order if offset] + [0]
+
     def gather_step(hops):
         for part in range(parts):
 
@@ -280,7 +283,7 @@
     near_select = one_hot(LANES, near_slots)
     near_labels = label_row(jnp.where(near_mine, near_targets - first + 1, 0), near_select)
     near_owned = times(near_select, near).astype(jnp.bfloat16)
-    for offset in range(naux - 1, -1, -1):
+    for offset in send_order:
         fitted = times(one_hot(cols, near_targets - mirrored(column, offset) * cols), near).astype(jnp.bfloat16)
         near_fitted[offset] = fitted
         sent_near[offset, :near_rows] = crossed(near_owned, fitted)[:near_rows]
@@ -299,7 +302,7 @@
     far_labels = label_row(jnp.where(far_mine, far_targets - first + 1, 0), far_select_wide)
     far_owned = times(far_select, last).astype(jnp.bfloat16)
     top_row = lax.broadcasted_iota(jnp.int32, (LABEL_ROWS, LANES), 0) == 0
-    for offset in range(naux - 1, -1, -1):
+    for offset in send_order:
         shifted = far_targets - mirrored(column, offset) * cols
         inside = (shifted >= 0) & (shifted < cols)
         ranks = jnp.where(inside, far_ranks, -1)

time: 29.5 us -> 29.9 us (1.014)
  Pallas kernels: 27.8 us -> 28.2 us
    pallas_call x1, Pallas kernels: 27.8 us -> 28.2 us  [fused(): pl.pallas_call(functools.partial(exchange_kernel, npair, naux, parts), ou...]
where the time goes in v6:
time: 29.9 us; the launch traced here: 29.7 us
  Pallas kernels  28.2 us (94%)
  local copies, waits for them, and re-layouts  1.57 us (5%)
    pallas_call x1, Pallas kernels, fused(): pl.pallas_call(functools.partial(exchange_kernel, npair, naux, parts), ou...  28.2 us
    unnamed x1, local copies, waits for them, and re-layouts  1.57 us

profile of v6, /device:TPU:0, one launch (start us, length us, event | category | flops | bytes accessed | tf_op | source)
XLA Modules:
  0.0 29.7 jit_solution(1587841711862087302)
XLA Ops:
  0.0 28.2 %shard_map.64 = f32[256,128]{1,0:T(8,128)} custom-call(s32[1,6]{1,0:T(1,128)} %mu_hbm.1, s32[6,1,8]{2,1,0:T(1,128)} %bitcast.1, s32[64]{0:T(128)} %size_hbm.1, s32[64]{0:T(128)} %order_hbm.1, f32[6,16,16,128]{3,2,1,0:T(8,128)} %integrals_hbm.1, f32[64,16,64]{2,1,0:T(8,128)} %coeffs_hbm.1), custom_call_target="tpu_custom_call" | custom-call | tf_op jit(solution)/shard_map/pallas_call | solution.py:381
  28.2 1.6 %copy.8 = f32[256,128]{1,0:T(8,128)} copy(f32[256,128]{1,0:T(8,128)} %shard_map.64) | data formatting | bytes 262144
